TPU v7x, 32 devices: a whole 2x2x4 slice. The times are simulated.
32 devices in a mesh: fg: 4 (over y, core), sp: 8 (over z, x).
Axes of the slice: x: 2, y: 2, z: 4, core: 2. Of those that a mesh axis runs over, the one named last changes fastest.
Arguments:
- latent: bfloat16 [16, 64, 240, 256], P('fg', 'sp'), may hold values from -6 to 6
- temporal_weight: bfloat16 [3, 256, 1024], replicated, may hold values from -0.21875 to 0.21875
- temporal_bias: float32 [1024], replicated, may hold values from -4 to 4
- spatial_weight: bfloat16 [3, 3, 256, 128], replicated, may hold values from -0.125 to 0.125
- spatial_bias: float32 [128], replicated, may hold values from -4 to 4
- counts: int32 [4], replicated, may hold values from 1 to 16, 48 in all
Outputs:
- decoded: bfloat16 [64, 64, 240, 128], P('fg', 'sp')
Inputs may be any that keep to these rules, and one draw needn't show every extreme that they name: `counts`: some group holds 16.
All inputs are finite; a program needn't handle non-finite values.
Results may differ from a plain program's by a relative error of at most 0.0038.
Values may be sent and summed in bfloat16 or wider, within the bound.
A program may use at most 320 MiB of HBM per device.

v0:
```python
import functools

import jax
import jax.numpy as jnp
from jax import lax
from jax.experimental import pallas as pl
from jax.experimental.pallas import tpu as pltpu
from jax.sharding import PartitionSpec as P

F32, BF16 = jnp.float32, jnp.bfloat16
LIMIT = 58 * 1024 * 1024
MESH = pl.DeviceIdType.MESH
SENDS = ((0, 1), (0, -1), (1, 1), (1, -1), (1, 0))
NEIGHBOURS = tuple((f, s) for f in (-1, 0, 1) for s in (-1, 0, 1) if f or s)


def silu(pre):
    half = 0.5 * pre
    return half + half * jnp.tanh(half)


def fill_weights(sw_ref, w01, w2):
    depth, wide = sw_ref.shape[2], sw_ref.shape[3]
    zero = jnp.zeros((depth, wide), BF16)
    for dy in range(3):
        at = pl.ds(dy * depth, depth)
        w01[at, :wide] = sw_ref[dy, 0]
        w01[at, wide:] = sw_ref[dy, 1]
    for q in range(4):
        at = pl.ds(q * depth, depth)
        w2[at, :wide] = sw_ref[q, 2] if q < 3 else zero
        w2[at, wide:] = sw_ref[q - 1, 2] if q > 0 else zero


def activation(a, j, tw_ref, tb_ref):
    width = tw_ref.shape[1] // 4
    columns = pl.ds(pl.multiple_of(j * width, width), width)
    pre = jnp.dot(a, tw_ref[:, columns], preferred_element_type=F32) + tb_ref[:, columns]
    return silu(pre).astype(BF16)


def zero_rims(left, right, cols):
    n, _, wide = left.shape
    left[:, 0:8, :] = jnp.zeros((n, 8, wide), F32)
    right[:, cols:cols + 8, :] = jnp.zeros((n, 8, wide), F32)


def row_pair(row, cols, w01, w2, left, mid, right, sb_ref, p):
    wide = sb_ref.shape[1]
    taps = [row(q) for q in range(4)]
    a = jnp.concatenate([jnp.concatenate(taps[h:h + 3], axis=1) for h in range(2)], axis=0)
    r = jnp.dot(a, w01[...], preferred_element_type=F32)
    s = jnp.dot(jnp.concatenate(taps, axis=1), w2[...], preferred_element_type=F32)
    rows = []
    for h in range(2):
        left[2 * p + h, 8:8 + cols, :] = r[h * cols:(h + 1) * cols, :wide]
        right[2 * p + h, 0:cols, :] = s[:, h * wide:(h + 1) * wide]
        mid[2 * p + h] = r[h * cols:(h + 1) * cols, wide:]
        total = left[2 * p + h, 7:7 + cols, :] + mid[2 * p + h] + right[2 * p + h, 1:1 + cols, :] + sb_ref[...]
        rows.append(total.astype(BF16))
    return rows


def late_kernel(sizes, latent_ref, tw_ref, tb_ref, sw_ref, sb_ref, out_ref, halo_ref, edge_ref,
                lat, up, w01, w2, w3, left, mid, right, load_sem, send_sem, recv_sem):
    frames, rows, cols, width = latent_ref.shape
    wide = sb_ref.shape[1]
    fg, sp = lax.axis_index("fg"), lax.axis_index("sp")

    loads = [pltpu.make_async_copy(latent_ref.at[f], lat.at[f], load_sem.at[f]) for f in range(frames)]
    for load in loads:
        load.start()

    def there(by, back=False):
        f, s = (fg - by[0], sp - by[1]) if back else (fg + by[0], sp + by[1])
        return (f >= 0) & (f < sizes[0]) & (s >= 0) & (s < sizes[1])

    barrier = pltpu.get_barrier_semaphore()
    for by in NEIGHBOURS:
        @pl.when(there(by))
        def _():
            pl.semaphore_signal(barrier, inc=1, device_id=(fg + by[0], sp + by[1]), device_id_type=MESH)
    near = [1 + (at > 0).astype(jnp.int32) + (at < n - 1).astype(jnp.int32) for at, n in zip((fg, sp), sizes)]
    pl.semaphore_wait(barrier, near[0] * near[1] - 1)

    last, head = latent_ref.at[:, rows - 1], latent_ref.at[:, 0]
    tail = pl.ds(frames - 2, 2)
    sources = (last, head, latent_ref.at[tail, rows - 1], latent_ref.at[tail, 0], latent_ref.at[tail])
    own, corner = pl.ds(2, frames), pl.ds(0, 2)
    targets = (halo_ref.at[0, own], halo_ref.at[1, own], halo_ref.at[0, corner], halo_ref.at[1, corner], edge_ref)

    def sent(i):
        by = SENDS[i]
        return pltpu.make_async_remote_copy(
            src_ref=sources[i], dst_ref=targets[i], send_sem=send_sem.at[i], recv_sem=recv_sem.at[i],
            device_id=(fg + by[0], sp + by[1]), device_id_type=MESH,
        )

    for i, by in enumerate(SENDS):
        @pl.when(there(by))
        def _():
            sent(i).start()

    fill_weights(sw_ref, w01, w2)
    for dy in range(3):
        for dx in range(3):
            w3[dy * width:(dy + 1) * width, dx * wide:(dx + 1) * wide] = sw_ref[dy, dx]
    zero_rims(left, right, cols)
    for load in loads:
        load.wait()

    def inner(i, carry):
        l, j = i // 4, i % 4
        for t in range(0, rows, 2):
            a = jnp.concatenate([lat[l + k, t:t + 2].reshape(2 * cols, width) for k in range(3)], axis=1)
            up[i, t * cols:(t + 2) * cols, :] = activation(a, j, tw_ref, tb_ref)
        for p in range(rows // 2 - 1):
            row = lambda q: up[i, pl.ds((2 * p + q) * cols, cols), :]
            for h, value in enumerate(row_pair(row, cols, w01, w2, left, mid, right, sb_ref, p)):
                out_ref[i, 2 * p + 1 + h] = value
        return carry

    lax.fori_loop(0, 8, inner, 0)

    for i in range(2):
        @pl.when(there(SENDS[i], True))
        def _():
            sent(i).wait_recv()

    def rim(i, carry):
        l, j = i // 4, i % 4
        a = jnp.concatenate([halo_ref[:, 2 + l + k].reshape(2 * cols, width) for k in range(3)], axis=1)
        act = activation(a, j, tw_ref, tb_ref)
        zero = jnp.zeros((cols, width), BF16)
        row = lambda h: up[i, pl.ds(h * cols, cols), :]
        above = [jnp.where(sp > 0, act[:cols], zero), row(0), row(1)]
        below = [row(rows - 2), row(rows - 1), jnp.where(sp < sizes[1] - 1, act[cols:], zero)]
        a = jnp.concatenate([jnp.concatenate(above, axis=1), jnp.concatenate(below, axis=1)], axis=0)
        r = jnp.dot(a, w3[...], preferred_element_type=F32)
        for h in range(2):
            part = r[h * cols:(h + 1) * cols]
            left[h, 8:8 + cols, :] = part[:, :wide]
            right[h, 0:cols, :] = part[:, 2 * wide:]
            total = left[h, 7:7 + cols, :] + (part[:, wide:2 * wide] + sb_ref[...]) + right[h, 1:1 + cols, :]
            out_ref[i, h * (rows - 1)] = total.astype(BF16)
        return carry

    lax.fori_loop(0, 8, rim, 0)

    for i, by in enumerate(SENDS):
        if i >= 2:
            @pl.when(there(by, True))
            def _():
                sent(i).wait_recv()

        @pl.when(there(by))
        def _():
            sent(i).wait_send()


def late_call(sizes, latent, tw, tb, sw, sb):
    frames, rows, cols, width = latent.shape
    wide = sw.shape[3]
    vmem = pl.BlockSpec(memory_space=pltpu.VMEM)
    hbm = pl.BlockSpec(memory_space=pl.ANY)
    return pl.pallas_call(
        functools.partial(late_kernel, sizes),
        in_specs=[hbm] + [vmem] * 4,
        out_specs=[vmem, vmem, hbm],
        out_shape=[
            jax.ShapeDtypeStruct((8, rows, cols, wide), BF16),
            jax.ShapeDtypeStruct((2, frames + 2, cols, width), BF16),
            jax.ShapeDtypeStruct((2, rows, cols, width), BF16),
        ],
        scratch_shapes=[
            pltpu.VMEM((frames, rows, cols, width), BF16),
            pltpu.VMEM((8, rows * cols, width), BF16),
            pltpu.VMEM((3 * width, 2 * wide), BF16),
            pltpu.VMEM((4 * width, 2 * wide), BF16),
            pltpu.VMEM((3 * width, 3 * wide), BF16),
            pltpu.VMEM((rows, cols + 8, wide), F32),
            pltpu.VMEM((rows, cols, wide), F32),
            pltpu.VMEM((rows, cols + 8, wide), F32),
            pltpu.SemaphoreType.DMA((frames,)),
            pltpu.SemaphoreType.DMA((len(SENDS),)),
            pltpu.SemaphoreType.DMA((len(SENDS),)),
        ],
        compiler_params=pltpu.CompilerParams(
            collective_id=0, has_side_effects=True, vmem_limit_bytes=LIMIT
        ),
        cost_estimate=pl.CostEstimate(flops=18 * 10**9, bytes_accessed=16 * 10**6, transcendentals=5 * 10**6),
        name="late_frames",
    )(latent, tw, tb, sw, sb)


def early_kernel(counts_ref, edge_ref, latent_ref, halo_ref, late_ref, tw_ref, tb_ref, sw_ref, sb_ref, out_ref,
                 x_ref, up, w01, w2, left, mid, right):
    rows, cols, width = latent_ref.shape[1:]
    fg, sp = lax.axis_index("fg"), lax.axis_index("sp")
    last_sp = lax.axis_size("sp") - 1
    l, j = pl.program_id(0), pl.program_id(1)
    step = 4 * l + j

    @pl.when(step == 0)
    def _():
        fill_weights(sw_ref, w01, w2)
        zero_rims(left, right, cols)

    def put(k, at, frame):
        x_ref[at * cols:at * cols + frame.shape[0], k * width:(k + 1) * width] = frame

    for at in range(2):
        @pl.when((l == at) & (j == 0))
        def _():
            for k in range(3):
                source = at + k - 2
                top, bottom = halo_ref[0, source + 2], halo_ref[1, source + 2]
                if source < 0:
                    body = edge_ref[source + 2].reshape(rows * cols, width)
                    top, body, bottom = (jnp.where(fg > 0, a, jnp.zeros_like(a)) for a in (top, body, bottom))
                else:
                    body = latent_ref[source].reshape(rows * cols, width)
                put(k, 0, top)
                put(k, 1, body)
                put(k, rows + 1, bottom)

    limit = counts_ref[fg]
    valid = step < limit

    @pl.when(valid)
    def _():
        for t in range(0, rows + 2, 2):
            at = pl.ds(t * cols, 2 * cols)
            up[at, :] = activation(x_ref[at, :], j, tw_ref, tb_ref)

        @pl.when(sp == 0)
        def _():
            up[0:cols, :] = jnp.zeros((cols, width), BF16)

        @pl.when(sp == last_sp)
        def _():
            up[(rows + 1) * cols:, :] = jnp.zeros((cols, width), BF16)

        for p in range(rows // 2):
            row = lambda q: up[pl.ds((2 * p + q) * cols, cols), :]
            for h, value in enumerate(row_pair(row, cols, w01, w2, left, mid, right, sb_ref, p)):
                out_ref[0, 0, 2 * p + h] = value

    @pl.when(jnp.logical_not(valid))
    def _():
        out_ref[0] = jnp.zeros(out_ref.shape[1:], BF16)

    @pl.when(step + 8 < limit)
    def _():
        out_ref[1] = late_ref[...]

    @pl.when(step + 8 >= limit)
    def _():
        out_ref[1] = jnp.zeros(out_ref.shape[1:], BF16)


def early_call(counts, edge, latent, halo, late, tw, tb, sw, sb):
    frames, rows, cols, width = latent.shape
    wide = sw.shape[3]
    whole = lambda a: pl.BlockSpec(a.shape, lambda l, j: (0,) * a.ndim)
    out = pl.pallas_call(
        early_kernel,
        grid=(2, 4),
        in_specs=[
            pl.BlockSpec(memory_space=pltpu.SMEM),
            whole(edge),
            pl.BlockSpec((2, rows, cols, width), lambda l, j: (0, 0, 0, 0)),
            whole(halo),
            pl.BlockSpec((1, rows, cols, wide), lambda l, j: (4 * l + j, 0, 0, 0)),
        ]
        + [whole(a) for a in (tw, tb, sw, sb)],
        out_specs=pl.BlockSpec((2, 1, rows, cols, wide), lambda l, j: (0, 4 * l + j, 0, 0, 0)),
        out_shape=jax.ShapeDtypeStruct((2, 8, rows, cols, wide), BF16),
        scratch_shapes=[
            pltpu.VMEM(((rows + 2) * cols, 3 * width), BF16),
            pltpu.VMEM(((rows + 2) * cols, width), BF16),
            pltpu.VMEM((3 * width, 2 * wide), BF16),
            pltpu.VMEM((4 * width, 2 * wide), BF16),
            pltpu.VMEM((rows, cols + 8, wide), F32),
            pltpu.VMEM((rows, cols, wide), F32),
            pltpu.VMEM((rows, cols + 8, wide), F32),
        ],
        compiler_params=pltpu.CompilerParams(
            dimension_semantics=("arbitrary", "arbitrary"), vmem_limit_bytes=LIMIT
        ),
        cost_estimate=pl.CostEstimate(flops=18 * 10**9, bytes_accessed=20 * 10**6, transcendentals=5 * 10**6),
        name="early_frames",
    )(counts, edge, latent, halo, late, tw, tb, sw, sb)
    return out.reshape(16, rows, cols, wide)


def on_device(sizes, latent, temporal_weight, temporal_bias, spatial_weight, spatial_bias, counts):
    width = latent.shape[3]
    tw = temporal_weight.reshape(3 * width, 4 * width)
    args = (tw, temporal_bias.reshape(1, -1), spatial_weight, spatial_bias.reshape(1, -1))
    late, halo, edge = late_call(sizes, latent, *args)
    return early_call(counts, edge, latent, halo, late, *args)


def solution(mesh):
    sizes = (mesh.shape["fg"], mesh.shape["sp"])
    return jax.shard_map(
        functools.partial(on_device, sizes),
        mesh=mesh,
        in_specs=(P("fg", "sp", None, None), P(), P(), P(), P(), P()),
        out_specs=P("fg", "sp", None, None),
        check_vma=False,
    )
```

profile of v0, /device:TPU:17, one launch (start us, length us, event | category | flops | bytes accessed | tf_op | source)
XLA Modules:
  0.0 72.4 jit_solution(6126938203456015645)
XLA Ops:
  0.0 41.8 %late_frames.1 = (bf16[8,8,240,128]{3,2,1,0:T(8,128)(2,1)}, bf16[2,6,240,256]{3,2,1,0:T(8,128)(2,1)}, bf16[2,8,240,256]{3,2,1,0:T(8,128)(2,1)}) custom-call(bf16[4,8,240,256]{3,2,1,0:T(8,128)(2,1)} %latent_ref.3, bf16[768,1024]{1,0:T(8,128)(2,1)} %bitcast.4, f32[1,1024]{1,0:T(1,128)} %bitcast.6, bf16[3,3,256,128]{3,2,1,0:T(8,128)(2,1)} %sw_ref.3, ...), custom_call_target="tpu_custom_call" | custom-call | flops 17999998976 | bytes 16000000 | tf_op jit(solution)/shard_map/late_frames/pallas_call | solution.py:166
  41.8 30.6 %early_frames.1 = bf16[2,8,8,240,128]{4,3,2,1,0:T(8,128)(2,1)} custom-call(s32[4]{0:T(128)} %counts_ref.1, bf16[2,8,240,256]{3,2,1,0:T(8,128)(2,1)} %get-tuple-element.8.edge_ref, bf16[4,8,240,256]{3,2,1,0:T(8,128)(2,1)} %latent_ref.3, bf16[2,6,240,256]{3,2,1,0:T(8,128)(2,1)} %get-tuple-element.9.halo_ref, ...), custom_call_target="tpu_custom_call" | custom-call | flops 17999998976 | bytes 20000000 | tf_op jit(solution)/shard_map/early_frames/pallas_call | solution.py:266
where the time goes:
time: 72.6 us; the launch traced here: 72.4 us
  Pallas kernels  72.4 us (100%)
    pallas_call x1, Pallas kernels, late_call(): pl.pallas_call(functools.partial(late_kernel, sizes), in_specs=[hbm] + [v...  41.8 us
    pallas_call x1, Pallas kernels, early_call(): pl.pallas_call(early_kernel, grid=(2, 4), in_specs=[pl.BlockSpec(memory_s...  30.6 us

commit v1 on v0

v1 whole, which is shorter than its diff:
```python
import functools

import jax
import jax.numpy as jnp
from jax import lax
from jax.experimental import pallas as pl
from jax.experimental.pallas import tpu as pltpu
from jax.sharding import PartitionSpec as P

F32, BF16 = jnp.float32, jnp.bfloat16
LIMIT = 46 * 1024 * 1024
MESH = pl.DeviceIdType.MESH
SENDS = ((0, 1), (0, -1), (1, 0), (1, 0), (1, 0), (1, 0))
NEIGHBOURS = ((0, 1), (0, -1), (1, 0), (-1, 0))


def silu(pre):
    half = 0.5 * pre
    return half + half * jnp.tanh(half)


def fill_weights(sw_ref, w01, w2):
    depth, wide = sw_ref.shape[2], sw_ref.shape[3]
    zero = jnp.zeros((depth, wide), BF16)
    for dy in range(3):
        at = pl.ds(dy * depth, depth)
        w01[at, :wide] = sw_ref[dy, 0]
        w01[at, wide:] = sw_ref[dy, 1]
    for q in range(4):
        at = pl.ds(q * depth, depth)
        w2[at, :wide] = sw_ref[q, 2] if q < 3 else zero
        w2[at, wide:] = sw_ref[q - 1, 2] if q > 0 else zero


def activation(a, j, tw_ref, tb_ref):
    width = tw_ref.shape[1] // 4
    columns = pl.ds(pl.multiple_of(j * width, width), width)
    pre = jnp.dot(a, tw_ref[:, columns], preferred_element_type=F32) + tb_ref[:, columns]
    return silu(pre).astype(BF16)


def zero_rims(left, right, cols):
    n, _, wide = left.shape
    left[:, 0:8, :] = jnp.zeros((n, 8, wide), F32)
    right[:, cols:cols + 8, :] = jnp.zeros((n, 8, wide), F32)


def row_pair(row, cols, w01, w2, left, mid, right, sb_ref, p):
    wide = sb_ref.shape[1]
    taps = [row(q) for q in range(4)]
    a = jnp.concatenate([jnp.concatenate(taps[h:h + 3], axis=1) for h in range(2)], axis=0)
    r = jnp.dot(a, w01[...], preferred_element_type=F32)
    s = jnp.dot(jnp.concatenate(taps, axis=1), w2[...], preferred_element_type=F32)
    rows = []
    for h in range(2):
        left[2 * p + h, 8:8 + cols, :] = r[h * cols:(h + 1) * cols, :wide]
        right[2 * p + h, 0:cols, :] = s[:, h * wide:(h + 1) * wide]
        mid[2 * p + h] = r[h * cols:(h + 1) * cols, wide:]
        total = left[2 * p + h, 7:7 + cols, :] + mid[2 * p + h] + right[2 * p + h, 1:1 + cols, :] + sb_ref[...]
        rows.append(total.astype(BF16))
    return rows


def frames_kernel(sizes, latent_ref, tw_ref, tb_ref, sw_ref, sb_ref, out_ref,
                  x, halo, up, tw, sw, w01, w2, w3, left, mid, right, load_sem, send_sem, recv_sem):
    frames, rows, cols, width = latent_ref.shape
    wide = sb_ref.shape[1]
    fg, sp = lax.axis_index("fg"), lax.axis_index("sp")
    last_fg, last_sp = sizes[0] - 1, sizes[1] - 1

    def there(by, back=False):
        f, s = (fg - by[0], sp - by[1]) if back else (fg + by[0], sp + by[1])
        return (f >= 0) & (f <= last_fg) & (s >= 0) & (s <= last_sp)

    barrier = pltpu.get_barrier_semaphore()
    for by in NEIGHBOURS:
        @pl.when(there(by))
        def _():
            pl.semaphore_signal(barrier, inc=1, device_id=(fg + by[0], sp + by[1]), device_id_type=MESH)

    loads = [pltpu.make_async_copy(latent_ref.at[f], x.at[2 + f], load_sem.at[f]) for f in range(frames)]
    loads.append(pltpu.make_async_copy(tw_ref, tw, load_sem.at[frames]))
    loads.append(pltpu.make_async_copy(sw_ref, sw, load_sem.at[frames + 1]))
    for load in loads:
        load.start()

    near = [(at > 0).astype(jnp.int32) + (at < n).astype(jnp.int32) for at, n in ((fg, last_fg), (sp, last_sp))]
    pl.semaphore_wait(barrier, near[0] + near[1])

    own, tail, before = pl.ds(2, frames), pl.ds(frames, 2), pl.ds(0, 2)
    sources = (latent_ref.at[:, rows - 1], latent_ref.at[:, 0], latent_ref.at[frames - 1], latent_ref.at[frames - 2],
               halo.at[0, tail], halo.at[1, tail])
    targets = (halo.at[0, own], halo.at[1, own], x.at[1], x.at[0], halo.at[0, before], halo.at[1, before])

    def sent(i):
        by = SENDS[i]
        return pltpu.make_async_remote_copy(
            src_ref=sources[i], dst_ref=targets[i], send_sem=send_sem.at[i], recv_sem=recv_sem.at[i],
            device_id=(fg + by[0], sp + by[1]), device_id_type=MESH,
        )

    above, below = sp > 0, sp < last_sp
    sends = [there(by) for by in SENDS[:4]] + [(fg < last_fg) & above, (fg < last_fg) & below]
    arrives = [there(by, True) for by in SENDS[:4]] + [(fg > 0) & above, (fg > 0) & below]

    def start(*which):
        for i in which:
            @pl.when(sends[i])
            def _():
                sent(i).start()

    def arrived(*which):
        for i in which:
            @pl.when(arrives[i])
            def _():
                sent(i).wait_recv()

    start(0, 1, 2, 3)

    @pl.when(fg == 0)
    def _():
        x[0:2] = jnp.zeros((2, rows, cols, width), BF16)
        halo[:, 0:2] = jnp.zeros((2, 2, cols, width), BF16)

    for side, there_is in enumerate((above, below)):
        @pl.when(jnp.logical_not(there_is))
        def _():
            halo[side] = jnp.zeros((frames + 2, cols, width), BF16)

    zero_rims(left, right, cols)
    for load in loads[::-1]:
        load.wait()
    fill_weights(sw, w01, w2)
    for dy in range(3):
        for dx in range(3):
            w3[dy * width:(dy + 1) * width, dx * wide:(dx + 1) * wide] = sw[dy, dx]

    def inner(i, carry):
        l, j = i // 4, i % 4
        for t in range(0, rows, 2):
            a = jnp.concatenate([x[l + k, t:t + 2].reshape(2 * cols, width) for k in range(3)], axis=1)
            up[i, t * cols:(t + 2) * cols, :] = activation(a, j, tw, tb_ref)
        for p in range(rows // 2 - 1):
            row = lambda q: up[i, pl.ds((2 * p + q) * cols, cols), :]
            for h, value in enumerate(row_pair(row, cols, w01, w2, left, mid, right, sb_ref, p)):
                out_ref[i, 2 * p + 1 + h] = value
        return carry

    def rim(i, carry):
        l, j = i // 4, i % 4
        a = jnp.concatenate([halo[:, l + k].reshape(2 * cols, width) for k in range(3)], axis=1)
        act = activation(a, j, tw, tb_ref)
        zero = jnp.zeros((cols, width), BF16)
        row = lambda h: up[i, pl.ds(h * cols, cols), :]
        first = [jnp.where(above, act[:cols], zero), row(0), row(1)]
        final = [row(rows - 2), row(rows - 1), jnp.where(below, act[cols:], zero)]
        a = jnp.concatenate([jnp.concatenate(first, axis=1), jnp.concatenate(final, axis=1)], axis=0)
        r = jnp.dot(a, w3[...], preferred_element_type=F32)
        for h in range(2):
            part = r[h * cols:(h + 1) * cols]
            left[h, 8:8 + cols, :] = part[:, :wide]
            right[h, 0:cols, :] = part[:, 2 * wide:]
            total = left[h, 7:7 + cols, :] + (part[:, wide:2 * wide] + sb_ref[...]) + right[h, 1:1 + cols, :]
            out_ref[i, h * (rows - 1)] = total.astype(BF16)
        return carry

    lax.fori_loop(8, 16, inner, 0)
    arrived(2)
    lax.fori_loop(4, 8, inner, 0)
    arrived(0, 1)
    start(4, 5)
    lax.fori_loop(8, 16, rim, 0)
    arrived(3)
    lax.fori_loop(0, 4, inner, 0)
    arrived(4, 5)
    lax.fori_loop(0, 8, rim, 0)

    for i in range(len(SENDS)):
        @pl.when(sends[i])
        def _():
            sent(i).wait_send()


def frames_call(sizes, latent, tw, tb, sw, sb):
    frames, rows, cols, width = latent.shape
    wide = sw.shape[3]
    vmem = pl.BlockSpec(memory_space=pltpu.VMEM)
    hbm = pl.BlockSpec(memory_space=pl.ANY)
    return pl.pallas_call(
        functools.partial(frames_kernel, sizes),
        in_specs=[hbm, hbm, vmem, hbm, vmem],
        out_specs=vmem,
        out_shape=pltpu.VMEM((4 * frames, rows, cols, wide), BF16),
        scratch_shapes=[
            pltpu.VMEM((frames + 2, rows, cols, width), BF16),
            pltpu.VMEM((2, frames + 2, cols, width), BF16),
            pltpu.VMEM((4 * frames, rows * cols, width), BF16),
            pltpu.VMEM(tw.shape, BF16),
            pltpu.VMEM(sw.shape, BF16),
            pltpu.VMEM((3 * width, 2 * wide), BF16),
            pltpu.VMEM((4 * width, 2 * wide), BF16),
            pltpu.VMEM((3 * width, 3 * wide), BF16),
            pltpu.VMEM((rows, cols + 8, wide), F32),
            pltpu.VMEM((rows, cols, wide), F32),
            pltpu.VMEM((rows, cols + 8, wide), F32),
            pltpu.SemaphoreType.DMA((frames + 2,)),
            pltpu.SemaphoreType.DMA((len(SENDS),)),
            pltpu.SemaphoreType.DMA((len(SENDS),)),
        ],
        compiler_params=pltpu.CompilerParams(
            collective_id=0, has_side_effects=True, vmem_limit_bytes=LIMIT
        ),
        cost_estimate=pl.CostEstimate(flops=36 * 10**9, bytes_accessed=16 * 10**6, transcendentals=10**7),
        name="frames",
    )(latent, tw, tb, sw, sb)


def flush_kernel(counts_ref, decoded_ref, out_ref, zero, sem):
    limit = counts_ref[lax.axis_index("fg")]
    zero[...] = jnp.zeros(zero.shape, BF16)
    count = decoded_ref.shape[0]
    copies = [pltpu.make_async_copy(decoded_ref.at[f], out_ref.at[f], sem.at[f]) for f in range(count)]
    for f, copy in enumerate(copies):
        pl.when(f < limit)(copy.start)
        pl.when(f >= limit)(pltpu.make_async_copy(zero, out_ref.at[f], sem.at[f]).start)
    for copy in copies:
        copy.wait()


def flush_call(counts, decoded):
    return pl.pallas_call(
        flush_kernel,
        in_specs=[pl.BlockSpec(memory_space=pltpu.SMEM), pl.BlockSpec(memory_space=pltpu.VMEM)],
        out_specs=pl.BlockSpec(memory_space=pl.ANY),
        out_shape=jax.ShapeDtypeStruct(decoded.shape, BF16),
        scratch_shapes=[pltpu.VMEM(decoded.shape[1:], BF16), pltpu.SemaphoreType.DMA((decoded.shape[0],))],
        compiler_params=pltpu.CompilerParams(vmem_limit_bytes=16 * 1024 * 1024),
        cost_estimate=pl.CostEstimate(flops=0, bytes_accessed=16 * 10**6, transcendentals=0),
        name="flush",
    )(counts, decoded)


def on_device(sizes, latent, temporal_weight, temporal_bias, spatial_weight, spatial_bias, counts):
    width = latent.shape[3]
    tw = temporal_weight.reshape(3 * width, 4 * width)
    args = (tw, temporal_bias.reshape(1, -1), spatial_weight, spatial_bias.reshape(1, -1))
    return flush_call(counts, frames_call(sizes, latent, *args))


def solution(mesh):
    sizes = (mesh.shape["fg"], mesh.shape["sp"])
    return jax.shard_map(
        functools.partial(on_device, sizes),
        mesh=mesh,
        in_specs=(P("fg", "sp", None, None), P(), P(), P(), P(), P()),
        out_specs=P("fg", "sp", None, None),
        check_vma=False,
    )
```

time: 72.6 us -> 54.5 us (0.75)
  Pallas kernels: 72.4 us -> 52.5 us
  local copies, waits for them, and re-layouts: 0 us -> 1.34 us
    pallas_call x2, Pallas kernels: 72.4 us -> 52.5 us  [the longest x1 48.7 us: frames_call(): pl.pallas_call(functools.partial(frames_kernel, sizes), in_specs=[hbm, hb...]
    unnamed x0 -> x6, local copies, waits for them, and re-layouts: none -> 1.34 us
where the time goes in v1:
time: 54.5 us; the launch traced here: 53.9 us
  Pallas kernels  52.5 us (96%)
  local copies, waits for them, and re-layouts  1.34 us (2%)
    pallas_call x1, Pallas kernels, frames_call(): pl.pallas_call(functools.partial(frames_kernel, sizes), in_specs=[hbm, hb...  48.7 us
    pallas_call x1, Pallas kernels, flush_call(): pl.pallas_call(flush_kernel, in_specs=[pl.BlockSpec(memory_space=pltpu.SM...  3.81 us
    unnamed x6, local copies, waits for them, and re-layouts  1.34 us

profile of v1, /device:TPU:17, one launch (start us, length us, event | category | flops | bytes accessed | tf_op | source)
XLA Modules:
  0.0 53.9 jit_solution(2942710040111726262)
XLA Ops:
  0.0 0.0 copy-start.1
  0.0 0.7 %copy-done.1 = f32[1024]{0:T(1024)S(1)} copy-done((f32[1024]{0:T(1024)S(1)}, f32[1024]{0:T(1024)}, u32[]{:S(2)}) %copy-start.1) | copy-done | bytes 4120
  0.7 0.0 copy-start.2
  0.7 0.7 %copy-done.2 = f32[128]{0:T(128)S(1)} copy-done((f32[128]{0:T(128)S(1)}, f32[128]{0:T(128)}, u32[]{:S(2)}) %copy-start.2) | copy-done | bytes 536
  1.3 0.0 copy-start
  1.3 48.7 %frames.1.decoded_ref = bf16[16,8,240,128]{3,2,1,0:T(8,128)(2,1)S(1)} custom-call(bf16[4,8,240,256]{3,2,1,0:T(8,128)(2,1)} %latent_ref.1, bf16[768,1024]{1,0:T(8,128)(2,1)} %bitcast.5, f32[1,1024]{1,0:T(1,128)S(1)} %bitcast.3, bf16[3,3,256,128]{3,2,1,0:T(8,128)(2,1)} %sw_ref.1, f32[1,128]{1,0:T(1,128)S(1)} %bitcast.4), custom_call_target="tpu_custom_call" | custom-call | flops 35999997952 | bytes 16000000 | tf_op jit(solution)/shard_map/frames/pallas_call | solution.py:189
  50.1 0.0 copy-done
  50.1 3.8 %flush.1 = bf16[16,8,240,128]{3,2,1,0:T(8,128)(2,1)} custom-call(s32[4]{0:T(128)S(1)} %copy-done, bf16[16,8,240,128]{3,2,1,0:T(8,128)(2,1)S(1)} %frames.1.decoded_ref), custom_call_target="tpu_custom_call" | custom-call | bytes 16000000 | tf_op jit(solution)/shard_map/flush/pallas_call | solution.py:231
Async XLA Ops:
  0.0 0.7 %copy-start.1 = (f32[1024]{0:T(1024)S(1)}, f32[1024]{0:T(1024)}, u32[]{:S(2)}) copy-start(f32[1024]{0:T(1024)} %param.8) | copy-start | bytes 12292
  0.7 0.7 %copy-start.2 = (f32[128]{0:T(128)S(1)}, f32[128]{0:T(128)}, u32[]{:S(2)}) copy-start(f32[128]{0:T(128)} %param.10) | copy-start | bytes 1540
  1.3 48.7 %copy-start = (s32[4]{0:T(128)S(1)}, s32[4]{0:T(128)}, u32[]{:S(2)}) copy-start(s32[4]{0:T(128)} %counts_ref.1) | copy-start | bytes 52

commit v2 on v1

v2 whole, which is shorter than its diff:
```python
import functools

import jax
import jax.numpy as jnp
from jax import lax
from jax.experimental import pallas as pl
from jax.experimental.pallas import tpu as pltpu
from jax.sharding import PartitionSpec as P

F32, BF16 = jnp.float32, jnp.bfloat16
LIMIT = 40 * 1024 * 1024
MESH = pl.DeviceIdType.MESH
SENDS = ((0, 1), (0, -1)) + ((1, 0),) * 6
NEIGHBOURS = ((0, 1), (0, -1), (1, 0), (-1, 0))


def silu(pre):
    half = 0.5 * pre
    return half + half * jnp.tanh(half)


def fill_weights(sw_ref, w01, w2):
    depth, wide = sw_ref.shape[2], sw_ref.shape[3]
    zero = jnp.zeros((depth, wide), BF16)
    for dy in range(3):
        at = pl.ds(dy * depth, depth)
        w01[at, :wide] = sw_ref[dy, 0]
        w01[at, wide:] = sw_ref[dy, 1]
    for q in range(4):
        at = pl.ds(q * depth, depth)
        w2[at, :wide] = sw_ref[q, 2] if q < 3 else zero
        w2[at, wide:] = sw_ref[q - 1, 2] if q > 0 else zero


def activation(a, j, tw_ref, tb_ref):
    width = tw_ref.shape[1] // 4
    columns = pl.ds(pl.multiple_of(j * width, width), width)
    pre = jnp.dot(a, tw_ref[:, columns], preferred_element_type=F32) + tb_ref[:, columns]
    return silu(pre).astype(BF16)


def zero_rims(left, right, cols):
    n, _, wide = left.shape
    left[:, 0:8, :] = jnp.zeros((n, 8, wide), F32)
    right[:, cols:cols + 8, :] = jnp.zeros((n, 8, wide), F32)


def row_pair(row, cols, w01, w2, left, mid, right, sb_ref, p):
    wide = sb_ref.shape[1]
    taps = [row(q) for q in range(4)]
    a = jnp.concatenate([jnp.concatenate(taps[h:h + 3], axis=1) for h in range(2)], axis=0)
    r = jnp.dot(a, w01[...], preferred_element_type=F32)
    s = jnp.dot(jnp.concatenate(taps, axis=1), w2[...], preferred_element_type=F32)
    rows = []
    for h in range(2):
        left[2 * p + h, 8:8 + cols, :] = r[h * cols:(h + 1) * cols, :wide]
        right[2 * p + h, 0:cols, :] = s[:, h * wide:(h + 1) * wide]
        mid[2 * p + h] = r[h * cols:(h + 1) * cols, wide:]
        total = left[2 * p + h, 7:7 + cols, :] + mid[2 * p + h] + right[2 * p + h, 1:1 + cols, :] + sb_ref[...]
        rows.append(total.astype(BF16))
    return rows


def frames_kernel(sizes, latent_ref, tw_ref, tb_ref, sw_ref, sb_ref,
                  out_ref, x, halo, tw, tb, sb, w01, w2,
                  up, sw, w3, left, mid, right, load_sem, send_sem, recv_sem):
    frames, rows, cols, width = latent_ref.shape
    wide = sb_ref.shape[1]
    fg, sp = lax.axis_index("fg"), lax.axis_index("sp")
    last_fg, last_sp = sizes[0] - 1, sizes[1] - 1

    def there(by, back=False):
        f, s = (fg - by[0], sp - by[1]) if back else (fg + by[0], sp + by[1])
        return (f >= 0) & (f <= last_fg) & (s >= 0) & (s <= last_sp)

    barrier = pltpu.get_barrier_semaphore()
    for by in NEIGHBOURS:
        @pl.when(there(by))
        def _():
            pl.semaphore_signal(barrier, inc=1, device_id=(fg + by[0], sp + by[1]), device_id_type=MESH)

    moves = [(sw_ref, sw), (tw_ref, tw), (tb_ref, tb), (sb_ref, sb)]
    moves += [(latent_ref.at[f], x.at[2 + f]) for f in range(frames)]
    loads = [pltpu.make_async_copy(source, target, load_sem.at[n]) for n, (source, target) in enumerate(moves)]
    for load in loads:
        load.start()

    zero_rims(left, right, cols)
    loads[0].wait()
    fill_weights(sw, w01, w2)
    for dy in range(3):
        for dx in range(3):
            w3[dy * width:(dy + 1) * width, dx * wide:(dx + 1) * wide] = sw[dy, dx]

    near = [(at > 0).astype(jnp.int32) + (at < n).astype(jnp.int32) for at, n in ((fg, last_fg), (sp, last_sp))]
    pl.semaphore_wait(barrier, near[0] + near[1])

    own = pl.ds(2, frames)
    sources = [latent_ref.at[:, rows - 1], latent_ref.at[:, 0], latent_ref.at[frames - 1], latent_ref.at[frames - 2]]
    targets = [halo.at[0, own], halo.at[1, own], x.at[1], x.at[0]]
    for k in (1, 0):
        sources += [halo.at[side, frames + k] for side in range(2)]
        targets += [halo.at[side, k] for side in range(2)]

    def sent(i):
        by = SENDS[i]
        return pltpu.make_async_remote_copy(
            src_ref=sources[i], dst_ref=targets[i], send_sem=send_sem.at[i], recv_sem=recv_sem.at[i],
            device_id=(fg + by[0], sp + by[1]), device_id_type=MESH,
        )

    above, below = sp > 0, sp < last_sp
    sends = [there(by) for by in SENDS[:4]] + [(fg < last_fg) & side for side in (above, below)] * 2
    arrives = [there(by, True) for by in SENDS[:4]] + [(fg > 0) & side for side in (above, below)] * 2

    def start(*which):
        for i in which:
            @pl.when(sends[i])
            def _():
                sent(i).start()

    def arrived(*which):
        for i in which:
            @pl.when(arrives[i])
            def _():
                sent(i).wait_recv()

    start(0, 1, 2, 3)

    @pl.when(fg == 0)
    def _():
        x[0:2] = jnp.zeros((2, rows, cols, width), BF16)
        halo[:, 0:2] = jnp.zeros((2, 2, cols, width), BF16)

    for side, there_is in enumerate((above, below)):
        @pl.when(jnp.logical_not(there_is))
        def _():
            halo[side] = jnp.zeros((frames + 2, cols, width), BF16)

    for load in loads[1:]:
        load.wait()

    def inner(n, carry):
        l = frames - 1 - n

        @pl.when(l == 1)
        def _():
            arrived(2)

        for j in range(4):
            i = 4 * l + j - 4
            for t in range(0, rows, 2):
                a = jnp.concatenate([x[l + k, t:t + 2].reshape(2 * cols, width) for k in range(3)], axis=1)
                up[i, t * cols:(t + 2) * cols, :] = activation(a, j, tw, tb)
            for p in range(rows // 2 - 1):
                row = lambda q: up[i, pl.ds((2 * p + q) * cols, cols), :]
                for h, value in enumerate(row_pair(row, cols, w01, w2, left, mid, right, sb, p)):
                    out_ref[i, 2 * p + 1 + h] = value
        return carry

    def rim(n, carry):
        l = frames - 1 - n

        @pl.when(l == 1)
        def _():
            arrived(4, 5)

        for j in range(4):
            i = 4 * l + j - 4
            a = jnp.concatenate([halo[:, l + k].reshape(2 * cols, width) for k in range(3)], axis=1)
            act = activation(a, j, tw, tb)
            zero = jnp.zeros((cols, width), BF16)
            row = lambda h: up[i, pl.ds(h * cols, cols), :]
            first = [jnp.where(above, act[:cols], zero), row(0), row(1)]
            final = [row(rows - 2), row(rows - 1), jnp.where(below, act[cols:], zero)]
            a = jnp.concatenate([jnp.concatenate(first, axis=1), jnp.concatenate(final, axis=1)], axis=0)
            r = jnp.dot(a, w3[...], preferred_element_type=F32)
            for h in range(2):
                part = r[h * cols:(h + 1) * cols]
                left[h, 8:8 + cols, :] = part[:, :wide]
                right[h, 0:cols, :] = part[:, 2 * wide:]
                total = left[h, 7:7 + cols, :] + (part[:, wide:2 * wide] + sb[...]) + right[h, 1:1 + cols, :]
                out_ref[i, h * (rows - 1)] = total.astype(BF16)
        return carry

    lax.fori_loop(0, frames - 1, inner, 0)
    arrived(0, 1)
    start(4, 5, 6, 7)
    lax.fori_loop(0, frames - 1, rim, 0)
    arrived(3, 6, 7)

    for i in range(len(SENDS)):
        @pl.when(sends[i])
        def _():
            sent(i).wait_send()


def frames_call(sizes, latent, tw, tb, sw, sb):
    frames, rows, cols, width = latent.shape
    wide = sw.shape[3]
    vmem = pl.BlockSpec(memory_space=pltpu.VMEM)
    hbm = pl.BlockSpec(memory_space=pl.ANY)
    out_shape = [
        pltpu.VMEM((4 * frames - 4, rows, cols, wide), BF16),
        pltpu.VMEM((frames + 2, rows, cols, width), BF16),
        pltpu.VMEM((2, frames + 2, cols, width), BF16),
        pltpu.VMEM(tw.shape, BF16),
        pltpu.VMEM(tb.shape, F32),
        pltpu.VMEM(sb.shape, F32),
        pltpu.VMEM((3 * width, 2 * wide), BF16),
        pltpu.VMEM((4 * width, 2 * wide), BF16),
    ]
    return pl.pallas_call(
        functools.partial(frames_kernel, sizes),
        in_specs=[hbm] * 5,
        out_specs=[vmem] * len(out_shape),
        out_shape=out_shape,
        scratch_shapes=[
            pltpu.VMEM((4 * frames - 4, rows * cols, width), BF16),
            pltpu.VMEM(sw.shape, BF16),
            pltpu.VMEM((3 * width, 3 * wide), BF16),
            pltpu.VMEM((rows, cols + 8, wide), F32),
            pltpu.VMEM((rows, cols, wide), F32),
            pltpu.VMEM((rows, cols + 8, wide), F32),
            pltpu.SemaphoreType.DMA((frames + 4,)),
            pltpu.SemaphoreType.DMA((len(SENDS),)),
            pltpu.SemaphoreType.DMA((len(SENDS),)),
        ],
        compiler_params=pltpu.CompilerParams(
            collective_id=0, has_side_effects=True, vmem_limit_bytes=LIMIT
        ),
        cost_estimate=pl.CostEstimate(flops=28 * 10**9, bytes_accessed=16 * 10**6, transcendentals=10**7),
        name="frames",
    )(latent, tw, tb, sw, sb)


def finish_kernel(counts_ref, late_ref, x, halo, tw, tb, sb, w01, w2, out_ref,
                  early, zero, up, left, mid, right, sem):
    rows, cols, width = x.shape[1:]
    fg, sp = lax.axis_index("fg"), lax.axis_index("sp")
    last_sp = lax.axis_size("sp") - 1
    limit = counts_ref[fg]
    zero[...] = jnp.zeros(zero.shape, BF16)

    def copy(source, f):
        return pltpu.make_async_copy(source, out_ref.at[f], sem.at[f])

    def leave(source, f):
        pl.when(f < limit)(copy(source, f).start)
        pl.when(f >= limit)(copy(zero, f).start)

    late = late_ref.shape[0]
    for f in range(late):
        leave(late_ref.at[f], 4 + f)
    zero_rims(left, right, cols)

    def rows_of(t, k):
        if t == 0:
            return jnp.concatenate([halo[0, k], x[k, 0]], axis=0)
        if t == rows:
            return jnp.concatenate([x[k, rows - 1], halo[1, k]], axis=0)
        return x[k, t - 1:t + 1].reshape(2 * cols, width)

    for j in range(4):
        for t in range(0, rows + 2, 2):
            a = jnp.concatenate([rows_of(t, k) for k in range(3)], axis=1)
            up[j, t * cols:(t + 2) * cols, :] = activation(a, j, tw, tb)

        @pl.when(sp == 0)
        def _():
            up[j, 0:cols, :] = jnp.zeros((cols, width), BF16)

        @pl.when(sp == last_sp)
        def _():
            up[j, (rows + 1) * cols:, :] = jnp.zeros((cols, width), BF16)

        for p in range(rows // 2):
            row = lambda q: up[j, pl.ds((2 * p + q) * cols, cols), :]
            for h, value in enumerate(row_pair(row, cols, w01, w2, left, mid, right, sb, p)):
                early[j, 2 * p + h] = value
        leave(early.at[j], j)

    for f in range(late + 4):
        copy(zero, f).wait()


def finish_call(counts, late, x, *args):
    _, rows, cols, wide = late.shape
    width = x.shape[3]
    shape = (late.shape[0] + 4, rows, cols, wide)
    vmem = pl.BlockSpec(memory_space=pltpu.VMEM)
    return pl.pallas_call(
        finish_kernel,
        in_specs=[pl.BlockSpec(memory_space=pltpu.SMEM)] + [vmem] * (2 + len(args)),
        out_specs=pl.BlockSpec(memory_space=pl.ANY),
        out_shape=jax.ShapeDtypeStruct(shape, BF16),
        scratch_shapes=[
            pltpu.VMEM((4,) + shape[1:], BF16),
            pltpu.VMEM(shape[1:], BF16),
            pltpu.VMEM((4, (rows + 2) * cols, width), BF16),
            pltpu.VMEM((rows, cols + 8, wide), F32),
            pltpu.VMEM((rows, cols, wide), F32),
            pltpu.VMEM((rows, cols + 8, wide), F32),
            pltpu.SemaphoreType.DMA((shape[0],)),
        ],
        compiler_params=pltpu.CompilerParams(vmem_limit_bytes=24 * 1024 * 1024),
        cost_estimate=pl.CostEstimate(flops=9 * 10**9, bytes_accessed=16 * 10**6, transcendentals=10**6),
        name="finish",
    )(counts, late, x, *args)


def on_device(sizes, latent, temporal_weight, temporal_bias, spatial_weight, spatial_bias, counts):
    width = latent.shape[3]
    tw = temporal_weight.reshape(3 * width, 4 * width)
    args = (tw, temporal_bias.reshape(1, -1), spatial_weight, spatial_bias.reshape(1, -1))
    return finish_call(counts, *frames_call(sizes, latent, *args))


def solution(mesh):
    sizes = (mesh.shape["fg"], mesh.shape["sp"])
    return jax.shard_map(
        functools.partial(on_device, sizes),
        mesh=mesh,
        in_specs=(P("fg", "sp", None, None), P(), P(), P(), P(), P()),
        out_specs=P("fg", "sp", None, None),
        check_vma=False,
    )
```

time: 54.5 us -> 51.4 us (0.943)
  Pallas kernels: 52.5 us -> 50.7 us
  local copies, waits for them, and re-layouts: 1.34 us -> 0.01 us
    pallas_call x2, Pallas kernels: 52.5 us -> 50.7 us  [the longest x1 36.9 us: frames_call(): pl.pallas_call(functools.partial(frames_kernel, sizes), in_specs=[hbm] *...]
    unnamed x6 -> x2, local copies, waits for them, and re-layouts: 1.34 us -> 0.01 us
where the time goes in v2:
time: 51.4 us; the launch traced here: 50.9 us
  Pallas kernels  50.7 us (99%)
    pallas_call x1, Pallas kernels, frames_call(): pl.pallas_call(functools.partial(frames_kernel, sizes), in_specs=[hbm] *...  36.9 us
    pallas_call x1, Pallas kernels, finish_call(): pl.pallas_call(finish_kernel, in_specs=[pl.BlockSpec(memory_space=pltpu.S...  13.8 us

profile of v2, /device:TPU:17, one launch (start us, length us, event | category | flops | bytes accessed | tf_op | source)
XLA Modules:
  0.0 50.9 jit_solution(18133023548641174023)
XLA Ops:
  0.0 0.0 copy-start
  0.0 36.9 %frames.1 = (bf16[12,8,240,128]{3,2,1,0:T(8,128)(2,1)S(1)}, bf16[6,8,240,256]{3,2,1,0:T(8,128)(2,1)S(1)}, bf16[2,6,240,256]{3,2,1,0:T(8,128)(2,1)S(1)}, bf16[768...) custom-call(bf16[4,8,240,256]{3,2,1,0:T(8,128)(2,1)} %latent_ref.1, ...), custom_call_target="tpu_custom_call" | custom-call | flops 28000000000 | bytes 16000000 | tf_op jit(solution)/shard_map/frames/pallas_call | solution.py:213
  36.9 0.0 copy-done
  36.9 13.8 %finish.1 = bf16[16,8,240,128]{3,2,1,0:T(8,128)(2,1)} custom-call(s32[4]{0:T(128)S(1)} %copy-done, bf16[12,8,240,128]{3,2,1,0:T(8,128)(2,1)S(1)} %get-tuple-element.13.late_ref, bf16[6,8,240,256]{3,2,1,0:T(8,128)(2,1)S(1)} %get-tuple-element.14.x, bf16[2,6,240,256]{3,2,1,0:T(8,128)(2,1)S(1)} %get-tuple-element.15.halo, ...), custom_call_target="tpu_custom_call" | custom-call | flops 8999999488 | bytes 16000000 | tf_op jit(solution)/shard_map/finish/pallas_call | solution.py:292
Async XLA Ops:
  0.0 36.9 %copy-start = (s32[4]{0:T(128)S(1)}, s32[4]{0:T(128)}, u32[]{:S(2)}) copy-start(s32[4]{0:T(128)} %counts_ref.1) | copy-start | bytes 52

commit v3 on v2

--- a/solution.py
+++ b/solution.py
@@ -85,6 +85,7 @@
     for load in loads:
         load.start()
 
+    out_ref[4 * frames - 4] = jnp.zeros(out_ref.shape[1:], BF16)
     zero_rims(left, right, cols)
     loads[0].wait()
     fill_weights(sw, w01, w2)
@@ -142,11 +143,6 @@
 
     def inner(n, carry):
         l = frames - 1 - n
-
-        @pl.when(l == 1)
-        def _():
-            arrived(2)
-
         for j in range(4):
             i = 4 * l + j - 4
             for t in range(0, rows, 2):
@@ -160,11 +156,6 @@
 
     def rim(n, carry):
         l = frames - 1 - n
-
-        @pl.when(l == 1)
-        def _():
-            arrived(4, 5)
-
         for j in range(4):
             i = 4 * l + j - 4
             a = jnp.concatenate([halo[:, l + k].reshape(2 * cols, width) for k in range(3)], axis=1)
@@ -183,10 +174,14 @@
                 out_ref[i, h * (rows - 1)] = total.astype(BF16)
         return carry
 
-    lax.fori_loop(0, frames - 1, inner, 0)
+    lax.fori_loop(0, frames - 2, inner, 0)
+    arrived(2)
+    inner(frames - 2, 0)
     arrived(0, 1)
     start(4, 5, 6, 7)
-    lax.fori_loop(0, frames - 1, rim, 0)
+    lax.fori_loop(0, frames - 2, rim, 0)
+    arrived(4, 5)
+    rim(frames - 2, 0)
     arrived(3, 6, 7)
 
     for i in range(len(SENDS)):
@@ -201,7 +196,7 @@
     vmem = pl.BlockSpec(memory_space=pltpu.VMEM)
     hbm = pl.BlockSpec(memory_space=pl.ANY)
     out_shape = [
-        pltpu.VMEM((4 * frames - 4, rows, cols, wide), BF16),
+        pltpu.VMEM((4 * frames - 3, rows, cols, wide), BF16),
         pltpu.VMEM((frames + 2, rows, cols, width), BF16),
         pltpu.VMEM((2, frames + 2, cols, width), BF16),
         pltpu.VMEM(tw.shape, BF16),
@@ -235,23 +230,19 @@
 
 
 def finish_kernel(counts_ref, late_ref, x, halo, tw, tb, sb, w01, w2, out_ref,
-                  early, zero, up, left, mid, right, sem):
+                  early, up, left, mid, right, sem):
     rows, cols, width = x.shape[1:]
     fg, sp = lax.axis_index("fg"), lax.axis_index("sp")
     last_sp = lax.axis_size("sp") - 1
     limit = counts_ref[fg]
-    zero[...] = jnp.zeros(zero.shape, BF16)
 
     def copy(source, f):
         return pltpu.make_async_copy(source, out_ref.at[f], sem.at[f])
 
-    def leave(source, f):
-        pl.when(f < limit)(copy(source, f).start)
-        pl.when(f >= limit)(copy(zero, f).start)
-
-    late = late_ref.shape[0]
+    late = late_ref.shape[0] - 1
     for f in range(late):
-        leave(late_ref.at[f], 4 + f)
+        copy(late_ref.at[jnp.where(4 + f < limit, f, late)], 4 + f).start()
+    early[4] = jnp.zeros(early.shape[1:], BF16)
     zero_rims(left, right, cols)
 
     def rows_of(t, k):
@@ -264,30 +255,27 @@
     for j in range(4):
         for t in range(0, rows + 2, 2):
             a = jnp.concatenate([rows_of(t, k) for k in range(3)], axis=1)
-            up[j, t * cols:(t + 2) * cols, :] = activation(a, j, tw, tb)
-
-        @pl.when(sp == 0)
-        def _():
-            up[j, 0:cols, :] = jnp.zeros((cols, width), BF16)
-
-        @pl.when(sp == last_sp)
-        def _():
-            up[j, (rows + 1) * cols:, :] = jnp.zeros((cols, width), BF16)
+            act = activation(a, j, tw, tb)
+            none = jnp.zeros((cols, width), BF16)
+            first = jnp.where(sp > 0, act[:cols], none) if t == 0 else act[:cols]
+            second = jnp.where(sp < last_sp, act[cols:], none) if t == rows else act[cols:]
+            up[j, t * cols:(t + 1) * cols, :] = first
+            up[j, (t + 1) * cols:(t + 2) * cols, :] = second
 
         for p in range(rows // 2):
             row = lambda q: up[j, pl.ds((2 * p + q) * cols, cols), :]
             for h, value in enumerate(row_pair(row, cols, w01, w2, left, mid, right, sb, p)):
                 early[j, 2 * p + h] = value
-        leave(early.at[j], j)
+        copy(early.at[jnp.where(j < limit, j, 4)], j).start()
 
     for f in range(late + 4):
-        copy(zero, f).wait()
+        copy(early.at[4], f).wait()
 
 
 def finish_call(counts, late, x, *args):
     _, rows, cols, wide = late.shape
     width = x.shape[3]
-    shape = (late.shape[0] + 4, rows, cols, wide)
+    shape = (late.shape[0] + 3, rows, cols, wide)
     vmem = pl.BlockSpec(memory_space=pltpu.VMEM)
     return pl.pallas_call(
         finish_kernel,
@@ -295,8 +283,7 @@
         out_specs=pl.BlockSpec(memory_space=pl.ANY),
         out_shape=jax.ShapeDtypeStruct(shape, BF16),
         scratch_shapes=[
-            pltpu.VMEM((4,) + shape[1:], BF16),
-            pltpu.VMEM(shape[1:], BF16),
+            pltpu.VMEM((5,) + shape[1:], BF16),
             pltpu.VMEM((4, (rows + 2) * cols, width), BF16),
             pltpu.VMEM((rows, cols + 8, wide), F32),
             pltpu.VMEM((rows, cols, wide), F32),

time: 51.4 us -> 49.1 us (0.955)
  Pallas kernels: 50.7 us -> 48.4 us
    pallas_call x1, Pallas kernels: 13.8 us -> 11.6 us  [finish_call(): pl.pallas_call(finish_kernel, in_specs=[pl.BlockSpec(memory_space=pltpu.S...]
where the time goes in v3:
time: 49.1 us; the launch traced here: 48.6 us
  Pallas kernels  48.4 us (99%)
    pallas_call x1, Pallas kernels, frames_call(): pl.pallas_call(functools.partial(frames_kernel, sizes), in_specs=[hbm] *...  36.8 us
    pallas_call x1, Pallas kernels, finish_call(): pl.pallas_call(finish_kernel, in_specs=[pl.BlockSpec(memory_space=pltpu.S...  11.6 us

profile of v3, /device:TPU:17, one launch (start us, length us, event | category | flops | bytes accessed | tf_op | source)
XLA Modules:
  0.0 48.6 jit_solution(2363856414854468673)
XLA Ops:
  0.0 0.0 copy-start
  0.0 36.8 %frames.1 = (bf16[13,8,240,128]{3,2,1,0:T(8,128)(2,1)S(1)}, bf16[6,8,240,256]{3,2,1,0:T(8,128)(2,1)S(1)}, bf16[2,6,240,256]{3,2,1,0:T(8,128)(2,1)S(1)}, bf16[768...) custom-call(bf16[4,8,240,256]{3,2,1,0:T(8,128)(2,1)} %latent_ref.1, ...), custom_call_target="tpu_custom_call" | custom-call | flops 28000000000 | bytes 16000000 | tf_op jit(solution)/shard_map/frames/pallas_call | solution.py:208
  36.9 0.0 copy-done
  36.9 11.6 %finish.1 = bf16[16,8,240,128]{3,2,1,0:T(8,128)(2,1)} custom-call(s32[4]{0:T(128)S(1)} %copy-done, bf16[13,8,240,128]{3,2,1,0:T(8,128)(2,1)S(1)} %get-tuple-element.13.late_ref, bf16[6,8,240,256]{3,2,1,0:T(8,128)(2,1)S(1)} %get-tuple-element.14.x, bf16[2,6,240,256]{3,2,1,0:T(8,128)(2,1)S(1)} %get-tuple-element.15.halo, ...), custom_call_target="tpu_custom_call" | custom-call | flops 8999999488 | bytes 16000000 | tf_op jit(solution)/shard_map/finish/pallas_call | solution.py:280
Async XLA Ops:
  0.0 36.9 %copy-start = (s32[4]{0:T(128)S(1)}, s32[4]{0:T(128)}, u32[]{:S(2)}) copy-start(s32[4]{0:T(128)} %counts_ref.1) | copy-start | bytes 52

commit v4 on v3

--- a/solution.py
+++ b/solution.py
@@ -15,7 +15,7 @@
 
 
 def silu(pre):
-    half = 0.5 * pre
+    half = pre
     return half + half * jnp.tanh(half)
 
 
@@ -63,7 +63,7 @@
 
 def frames_kernel(sizes, latent_ref, tw_ref, tb_ref, sw_ref, sb_ref,
                   out_ref, x, halo, tw, tb, sb, w01, w2,
-                  up, sw, w3, left, mid, right, load_sem, send_sem, recv_sem):
+                  up, edge, sw, w3, left, mid, right, load_sem, send_sem, recv_sem):
     frames, rows, cols, width = latent_ref.shape
     wide = sb_ref.shape[1]
     fg, sp = lax.axis_index("fg"), lax.axis_index("sp")
@@ -140,6 +140,8 @@
 
     for load in loads[1:]:
         load.wait()
+    tw[...] = tw[...] * 0.5
+    tb[...] = tb[...] * 0.5
 
     def inner(n, carry):
         l = frames - 1 - n
@@ -156,22 +158,37 @@
 
     def rim(n, carry):
         l = frames - 1 - n
-        for j in range(4):
-            i = 4 * l + j - 4
+
+        def temporal(j):
             a = jnp.concatenate([halo[:, l + k].reshape(2 * cols, width) for k in range(3)], axis=1)
             act = activation(a, j, tw, tb)
             zero = jnp.zeros((cols, width), BF16)
+            edge[j][:cols] = jnp.where(above, act[:cols], zero)
+            edge[j][cols:] = jnp.where(below, act[cols:], zero)
+
+        def spatial(j):
+            i = 4 * l + j - 4
             row = lambda h: up[i, pl.ds(h * cols, cols), :]
-            first = [jnp.where(above, act[:cols], zero), row(0), row(1)]
-            final = [row(rows - 2), row(rows - 1), jnp.where(below, act[cols:], zero)]
+            first = [edge[j][:cols], row(0), row(1)]
+            final = [row(rows - 2), row(rows - 1), edge[j][cols:]]
             a = jnp.concatenate([jnp.concatenate(first, axis=1), jnp.concatenate(final, axis=1)], axis=0)
             r = jnp.dot(a, w3[...], preferred_element_type=F32)
             for h in range(2):
                 part = r[h * cols:(h + 1) * cols]
-                left[h, 8:8 + cols, :] = part[:, :wide]
-                right[h, 0:cols, :] = part[:, 2 * wide:]
-                total = left[h, 7:7 + cols, :] + (part[:, wide:2 * wide] + sb[...]) + right[h, 1:1 + cols, :]
+                left[2 * j + h, 8:8 + cols, :] = part[:, :wide]
+                right[2 * j + h, 0:cols, :] = part[:, 2 * wide:]
+                here = part[:, wide:2 * wide] + sb[...]
+                total = left[2 * j + h, 7:7 + cols, :] + here + right[2 * j + h, 1:1 + cols, :]
                 out_ref[i, h * (rows - 1)] = total.astype(BF16)
+
+        temporal(0)
+        temporal(1)
+        spatial(0)
+        temporal(2)
+        spatial(1)
+        temporal(3)
+        spatial(2)
+        spatial(3)
         return carry
 
     lax.fori_loop(0, frames - 2, inner, 0)
@@ -212,6 +229,7 @@
         out_shape=out_shape,
         scratch_shapes=[
             pltpu.VMEM((4 * frames - 4, rows * cols, width), BF16),
+            [pltpu.VMEM((2 * cols, width), BF16)] * 4,
             pltpu.VMEM(sw.shape, BF16),
             pltpu.VMEM((3 * width, 3 * wide), BF16),
             pltpu.VMEM((rows, cols + 8, wide), F32),

time: 49.1 us -> 46.4 us (0.945)
  Pallas kernels: 48.4 us -> 45.7 us
    pallas_call x1, Pallas kernels: 36.8 us -> 34.4 us  [frames_call(): pl.pallas_call(functools.partial(frames_kernel, sizes), in_specs=[hbm] *...]
where the time goes in v4:
time: 46.4 us; the launch traced here: 45.8 us
  Pallas kernels  45.7 us (98%)
    pallas_call x1, Pallas kernels, frames_call(): pl.pallas_call(functools.partial(frames_kernel, sizes), in_specs=[hbm] *...  34.4 us
    pallas_call x1, Pallas kernels, finish_call(): pl.pallas_call(finish_kernel, in_specs=[pl.BlockSpec(memory_space=pltpu.S...  11.3 us

profile of v4, /device:TPU:17, one launch (start us, length us, event | category | flops | bytes accessed | tf_op | source)
XLA Modules:
  0.0 45.8 jit_solution(5756707417215871525)
XLA Ops:
  0.0 0.0 copy-start
  0.0 34.4 %frames.1 = (bf16[13,8,240,128]{3,2,1,0:T(8,128)(2,1)S(1)}, bf16[6,8,240,256]{3,2,1,0:T(8,128)(2,1)S(1)}, bf16[2,6,240,256]{3,2,1,0:T(8,128)(2,1)S(1)}, bf16[768...) custom-call(bf16[4,8,240,256]{3,2,1,0:T(8,128)(2,1)} %latent_ref.1, ...), custom_call_target="tpu_custom_call" | custom-call | flops 28000000000 | bytes 16000000 | tf_op jit(solution)/shard_map/frames/pallas_call | solution.py:225
  34.4 0.0 copy-done
  34.4 11.3 %finish.1 = bf16[16,8,240,128]{3,2,1,0:T(8,128)(2,1)} custom-call(s32[4]{0:T(128)S(1)} %copy-done, bf16[13,8,240,128]{3,2,1,0:T(8,128)(2,1)S(1)} %get-tuple-element.13.late_ref, bf16[6,8,240,256]{3,2,1,0:T(8,128)(2,1)S(1)} %get-tuple-element.14.x, bf16[2,6,240,256]{3,2,1,0:T(8,128)(2,1)S(1)} %get-tuple-element.15.halo, ...), custom_call_target="tpu_custom_call" | custom-call | flops 8999999488 | bytes 16000000 | tf_op jit(solution)/shard_map/finish/pallas_call | solution.py:298
Async XLA Ops:
  0.0 34.4 %copy-start = (s32[4]{0:T(128)S(1)}, s32[4]{0:T(128)}, u32[]{:S(2)}) copy-start(s32[4]{0:T(128)} %counts_ref.1) | copy-start | bytes 52

commit v5 on v4

--- a/solution.py
+++ b/solution.py
@@ -56,7 +56,7 @@
         left[2 * p + h, 8:8 + cols, :] = r[h * cols:(h + 1) * cols, :wide]
         right[2 * p + h, 0:cols, :] = s[:, h * wide:(h + 1) * wide]
         mid[2 * p + h] = r[h * cols:(h + 1) * cols, wide:]
-        total = left[2 * p + h, 7:7 + cols, :] + mid[2 * p + h] + right[2 * p + h, 1:1 + cols, :] + sb_ref[...]
+        total = pltpu.roll(left[2 * p + h], 1, 0)[8:] + mid[2 * p + h] + pltpu.roll(right[2 * p + h], cols + 7, 0)[:cols] + sb_ref[...]
         rows.append(total.astype(BF16))
     return rows
 
@@ -178,7 +178,7 @@
                 left[2 * j + h, 8:8 + cols, :] = part[:, :wide]
                 right[2 * j + h, 0:cols, :] = part[:, 2 * wide:]
                 here = part[:, wide:2 * wide] + sb[...]
-                total = left[2 * j + h, 7:7 + cols, :] + here + right[2 * j + h, 1:1 + cols, :]
+                total = pltpu.roll(left[2 * j + h], 1, 0)[8:] + here + pltpu.roll(right[2 * j + h], cols + 7, 0)[:cols]
                 out_ref[i, h * (rows - 1)] = total.astype(BF16)
 
         temporal(0)
@@ -255,7 +255,7 @@
     limit = counts_ref[fg]
 
     def copy(source, f):
-        return pltpu.make_async_copy(source, out_ref.at[f], sem.at[f])
+        return pltpu.make_async_copy(source, out_ref.at[f], sem)
 
     late = late_ref.shape[0] - 1
     for f in range(late):
@@ -286,8 +286,7 @@
                 early[j, 2 * p + h] = value
         copy(early.at[jnp.where(j < limit, j, 4)], j).start()
 
-    for f in range(late + 4):
-        copy(early.at[4], f).wait()
+    pltpu.make_async_copy(out_ref, out_ref, sem).wait()
 
 
 def finish_call(counts, late, x, *args):
@@ -306,7 +305,7 @@
             pltpu.VMEM((rows, cols + 8, wide), F32),
             pltpu.VMEM((rows, cols, wide), F32),
             pltpu.VMEM((rows, cols + 8, wide), F32),
-            pltpu.SemaphoreType.DMA((shape[0],)),
+            pltpu.SemaphoreType.DMA(()),
         ],
         compiler_params=pltpu.CompilerParams(vmem_limit_bytes=24 * 1024 * 1024),
         cost_estimate=pl.CostEstimate(flops=9 * 10**9, bytes_accessed=16 * 10**6, transcendentals=10**6),

time: 46.4 us -> 44.2 us (0.953)
  Pallas kernels: 45.7 us -> 43.9 us
    pallas_call x1, Pallas kernels: 34.4 us -> 33.2 us  [frames_call(): pl.pallas_call(functools.partial(frames_kernel, sizes), in_specs=[hbm] *...]
    pallas_call x1, Pallas kernels: 11.3 us -> 10.7 us  [finish_call(): pl.pallas_call(finish_kernel, in_specs=[pl.BlockSpec(memory_space=pltpu.S...]
where the time goes in v5:
time: 44.2 us; the launch traced here: 44.1 us
  Pallas kernels  43.9 us (99%)
    pallas_call x1, Pallas kernels, frames_call(): pl.pallas_call(functools.partial(frames_kernel, sizes), in_specs=[hbm] *...  33.2 us
    pallas_call x1, Pallas kernels, finish_call(): pl.pallas_call(finish_kernel, in_specs=[pl.BlockSpec(memory_space=pltpu.S...  10.7 us

profile of v5, /device:TPU:17, one launch (start us, length us, event | category | flops | bytes accessed | tf_op | source)
XLA Modules:
  0.0 44.1 jit_solution(9780169522998415227)
XLA Ops:
  0.0 0.0 copy-start
  0.0 33.2 %frames.1 = (bf16[13,8,240,128]{3,2,1,0:T(8,128)(2,1)S(1)}, bf16[6,8,240,256]{3,2,1,0:T(8,128)(2,1)S(1)}, bf16[2,6,240,256]{3,2,1,0:T(8,128)(2,1)S(1)}, bf16[768...) custom-call(bf16[4,8,240,256]{3,2,1,0:T(8,128)(2,1)} %latent_ref.1, ...), custom_call_target="tpu_custom_call" | custom-call | flops 28000000000 | bytes 16000000 | tf_op jit(solution)/shard_map/frames/pallas_call | solution.py:225
  33.2 0.0 copy-done
  33.2 10.7 %finish.1 = bf16[16,8,240,128]{3,2,1,0:T(8,128)(2,1)} custom-call(s32[4]{0:T(128)S(1)} %copy-done, bf16[13,8,240,128]{3,2,1,0:T(8,128)(2,1)S(1)} %get-tuple-element.13.late_ref, bf16[6,8,240,256]{3,2,1,0:T(8,128)(2,1)S(1)} %get-tuple-element.14.x, bf16[2,6,240,256]{3,2,1,0:T(8,128)(2,1)S(1)} %get-tuple-element.15.halo, ...), custom_call_target="tpu_custom_call" | custom-call | flops 8999999488 | bytes 16000000 | tf_op jit(solution)/shard_map/finish/pallas_call | solution.py:297
Async XLA Ops:
  0.0 33.2 %copy-start = (s32[4]{0:T(128)S(1)}, s32[4]{0:T(128)}, u32[]{:S(2)}) copy-start(s32[4]{0:T(128)} %counts_ref.1) | copy-start | bytes 52

commit v6 on v5

--- a/solution.py
+++ b/solution.py
@@ -55,8 +55,8 @@
     for h in range(2):
         left[2 * p + h, 8:8 + cols, :] = r[h * cols:(h + 1) * cols, :wide]
         right[2 * p + h, 0:cols, :] = s[:, h * wide:(h + 1) * wide]
-        mid[2 * p + h] = r[h * cols:(h + 1) * cols, wide:]
-        total = pltpu.roll(left[2 * p + h], 1, 0)[8:] + mid[2 * p + h] + pltpu.roll(right[2 * p + h], cols + 7, 0)[:cols] + sb_ref[...]
+        here = r[h * cols:(h + 1) * cols, wide:] + sb_ref[...]
+        total = pltpu.roll(left[2 * p + h], 1, 0)[8:] + here + pltpu.roll(right[2 * p + h], cols + 7, 0)[:cols]
         rows.append(total.astype(BF16))
     return rows
 
@@ -93,6 +93,11 @@
         for dx in range(3):
             w3[dy * width:(dy + 1) * width, dx * wide:(dx + 1) * wide] = sw[dy, dx]
 
+    for load in loads[1:4]:
+        load.wait()
+    tw[...] = tw[...] * 0.5
+    tb[...] = tb[...] * 0.5
+
     near = [(at > 0).astype(jnp.int32) + (at < n).astype(jnp.int32) for at, n in ((fg, last_fg), (sp, last_sp))]
     pl.semaphore_wait(barrier, near[0] + near[1])
 
@@ -138,10 +143,8 @@
         def _():
             halo[side] = jnp.zeros((frames + 2, cols, width), BF16)
 
-    for load in loads[1:]:
+    for load in loads[4:]:
         load.wait()
-    tw[...] = tw[...] * 0.5
-    tb[...] = tb[...] * 0.5
 
     def inner(n, carry):
         l = frames - 1 - n

time: 44.2 us -> 44.2 us (level)
  no operation moved by 1% of the time
where the time goes in v6:
time: 44.2 us; the launch traced here: 44 us
  Pallas kernels  43.8 us (99%)
    pallas_call x1, Pallas kernels, frames_call(): pl.pallas_call(functools.partial(frames_kernel, sizes), in_specs=[hbm] *...  33.2 us
    pallas_call x1, Pallas kernels, finish_call(): pl.pallas_call(finish_kernel, in_specs=[pl.BlockSpec(memory_space=pltpu.S...  10.6 us

profile of v6, /device:TPU:17, one launch (start us, length us, event | category | flops | bytes accessed | tf_op | source)
XLA Modules:
  0.0 44.0 jit_solution(9761720410525347207)
XLA Ops:
  0.0 0.0 copy-start
  0.0 33.2 %frames.1 = (bf16[13,8,240,128]{3,2,1,0:T(8,128)(2,1)S(1)}, bf16[6,8,240,256]{3,2,1,0:T(8,128)(2,1)S(1)}, bf16[2,6,240,256]{3,2,1,0:T(8,128)(2,1)S(1)}, bf16[768...) custom-call(bf16[4,8,240,256]{3,2,1,0:T(8,128)(2,1)} %latent_ref.1, ...), custom_call_target="tpu_custom_call" | custom-call | flops 28000000000 | bytes 16000000 | tf_op jit(solution)/shard_map/frames/pallas_call | solution.py:228
  33.2 0.0 copy-done
  33.2 10.6 %finish.1 = bf16[16,8,240,128]{3,2,1,0:T(8,128)(2,1)} custom-call(s32[4]{0:T(128)S(1)} %copy-done, bf16[13,8,240,128]{3,2,1,0:T(8,128)(2,1)S(1)} %get-tuple-element.13.late_ref, bf16[6,8,240,256]{3,2,1,0:T(8,128)(2,1)S(1)} %get-tuple-element.14.x, bf16[2,6,240,256]{3,2,1,0:T(8,128)(2,1)S(1)} %get-tuple-element.15.halo, ...), custom_call_target="tpu_custom_call" | custom-call | flops 8999999488 | bytes 16000000 | tf_op jit(solution)/shard_map/finish/pallas_call | solution.py:300
Async XLA Ops:
  0.0 33.2 %copy-start = (s32[4]{0:T(128)S(1)}, s32[4]{0:T(128)}, u32[]{:S(2)}) copy-start(s32[4]{0:T(128)} %counts_ref.1) | copy-start | bytes 52
